TPU v7x, 256 devices: a whole 4x4x8 slice. The times are simulated.
256 devices in a mesh: tm: 8 (over x, z_lo), space: 32 (over z_hi, y, core).
Axes of the slice: x: 4, y: 4, z: 8 (z_hi: 4, z_lo: 2; z = z_hi * 2 + z_lo), core: 2. Of those that a mesh axis runs over, the one named last changes fastest.
Arguments:
- snapshots: float32 [2048, 2, 131072], P('tm', None, 'space'), may hold values from -120 to 120
- quad_weights: float32 [131072], P('space'), may hold values from 0.25 to 4
Outputs:
- mode_blocks: float32 [8, 64, 2, 131072], P(None, 'tm', None, 'space')
- upper_factor: float32 [64, 2, 8, 8], P('tm')
All inputs are finite; a program needn't handle non-finite values.
Results may differ from a plain program's by a relative error of at most 0.00013.
Values sent between devices are 32-bit elements; how exact they have to be, the bound alone decides.
A program may use at most 128 MiB of HBM per device.

v0:
```python
import math

import jax
import jax.numpy as jnp
from jax import lax
from jax.sharding import PartitionSpec as P

NB = 8
NFFT = 256
KF = 64


def joined(part, axis, combine):
    gathered = jax.tree.map(lambda a: lax.all_gather(a, axis), part)

    def take(source):
        return jax.tree.map(lambda a: lax.dynamic_index_in_dim(a, source, 0, False), gathered)

    return lax.fori_loop(
        1, lax.axis_size(axis), lambda source, state: combine(state, take(source)), take(0)
    )


def dft_tables():
    column = jnp.arange(NFFT, dtype=jnp.int32)
    freqs = jnp.arange(KF, dtype=jnp.int32)
    window = 0.54 - 0.46 * jnp.cos(2.0 * math.pi * column.astype(jnp.float32) / NFFT)
    phase = (freqs[:, None] * column[None, :] % NFFT).astype(jnp.float32)
    angles = 2.0 * math.pi * phase / NFFT
    return (window[None, :] * jnp.cos(angles), window[None, :] * jnp.sin(angles))


def transform(centered, cos_tab, sin_tab):
    highest = lax.Precision.HIGHEST
    spec_re = jnp.einsum("kj,bjp->bkp", cos_tab, centered[:, :, 0], precision=highest) + jnp.einsum(
        "kj,bjp->bkp", sin_tab, centered[:, :, 1], precision=highest
    )
    spec_im = jnp.einsum("kj,bjp->bkp", cos_tab, centered[:, :, 1], precision=highest) - jnp.einsum(
        "kj,bjp->bkp", sin_tab, centered[:, :, 0], precision=highest
    )
    return jnp.stack([spec_re, spec_im], axis=2)


def local_gram(spectra, scaled):
    highest = lax.Precision.HIGHEST
    weighted = spectra * scaled
    gram_re = jnp.einsum(
        "afp,bfp->abf", weighted[:, :, 0], spectra[:, :, 0], precision=highest
    ) + jnp.einsum("afp,bfp->abf", weighted[:, :, 1], spectra[:, :, 1], precision=highest)
    gram_im = jnp.einsum(
        "afp,bfp->abf", weighted[:, :, 0], spectra[:, :, 1], precision=highest
    ) - jnp.einsum("afp,bfp->abf", weighted[:, :, 1], spectra[:, :, 0], precision=highest)
    return (gram_re, gram_im)


def factor_gram(fac_re, fac_im):
    highest = lax.Precision.HIGHEST
    gram_re = jnp.einsum("kaf,kbf->abf", fac_re, fac_re, precision=highest) + jnp.einsum(
        "kaf,kbf->abf", fac_im, fac_im, precision=highest
    )
    gram_im = jnp.einsum("kaf,kbf->abf", fac_re, fac_im, precision=highest) - jnp.einsum(
        "kaf,kbf->abf", fac_im, fac_re, precision=highest
    )
    return (gram_re, gram_im)


def stack_rows(table):
    return jnp.stack([jnp.stack(entries, 0) for entries in table], 0)


def cholesky_upper(gram_re, gram_im):
    size_n = gram_re.shape[0]
    zero_row = jnp.zeros_like(gram_re[0, 0])
    upper_re = [[zero_row] * size_n for row_i in range(size_n)]
    upper_im = [[zero_row] * size_n for row_i in range(size_n)]
    for j in range(size_n):
        pivot_sq = gram_re[j, j]
        for k in range(j):
            pivot_sq = pivot_sq - upper_re[k][j] * upper_re[k][j] - upper_im[k][j] * upper_im[k][j]
        pivot_root = jnp.sqrt(pivot_sq)
        upper_re[j][j] = pivot_root
        for i in range(j + 1, size_n):
            acc_re = gram_re[j, i]
            acc_im = gram_im[j, i]
            for k in range(j):
                acc_re = acc_re - (
                    upper_re[k][j] * upper_re[k][i] + upper_im[k][j] * upper_im[k][i]
                )
                acc_im = acc_im - (
                    upper_re[k][j] * upper_im[k][i] - upper_im[k][j] * upper_re[k][i]
                )
            upper_re[j][i] = acc_re / pivot_root
            upper_im[j][i] = acc_im / pivot_root
    return (stack_rows(upper_re), stack_rows(upper_im))


def combine_factors(left_pair, right_pair):
    left_re, left_im = factor_gram(left_pair[0], left_pair[1])
    right_re, right_im = factor_gram(right_pair[0], right_pair[1])
    return cholesky_upper(left_re + right_re, left_im + right_im)


def invert_upper(upper_re, upper_im):
    size_n = upper_re.shape[0]
    zero_row = jnp.zeros_like(upper_re[0, 0])
    inv_re = [[zero_row] * size_n for row_i in range(size_n)]
    inv_im = [[zero_row] * size_n for row_i in range(size_n)]
    for j in range(size_n):
        inv_re[j][j] = 1.0 / upper_re[j, j]
        for i in range(j - 1, -1, -1):
            acc_re = zero_row
            acc_im = zero_row
            for k in range(i + 1, j + 1):
                acc_re = acc_re + upper_re[i, k] * inv_re[k][j] - upper_im[i, k] * inv_im[k][j]
                acc_im = acc_im + upper_re[i, k] * inv_im[k][j] + upper_im[i, k] * inv_re[k][j]
            inv_re[i][j] = -acc_re / upper_re[i, i]
            inv_im[i][j] = -acc_im / upper_re[i, i]
    return (stack_rows(inv_re), stack_rows(inv_im))


def apply_inverse(spectra, inv_re, inv_im):
    highest = lax.Precision.HIGHEST
    mode_re = jnp.einsum("afp,abf->bfp", spectra[:, :, 0], inv_re, precision=highest) - jnp.einsum(
        "afp,abf->bfp", spectra[:, :, 1], inv_im, precision=highest
    )
    mode_im = jnp.einsum("afp,abf->bfp", spectra[:, :, 0], inv_im, precision=highest) + jnp.einsum(
        "afp,abf->bfp", spectra[:, :, 1], inv_re, precision=highest
    )
    return jnp.stack([mode_re, mode_im], axis=2)


def body(snapshots, quad_weights):
    cell_count = snapshots.shape[2]
    blocks_dev = snapshots.shape[0] // NFFT
    point_total = cell_count * lax.axis_size("space")
    block_total = jnp.sum(snapshots, axis=0)
    time_mean = lax.psum(block_total, "tm") / (NB * NFFT)
    centered = snapshots.reshape(blocks_dev, NFFT, 2, cell_count) - time_mean
    cos_tab, sin_tab = dft_tables()
    spectra = transform(centered, cos_tab, sin_tab)
    scaled = quad_weights / point_total
    owned_spec = lax.all_to_all(spectra, "tm", split_axis=1, concat_axis=0, tiled=True)
    gram_re, gram_im = local_gram(owned_spec, scaled)
    fac_re, fac_im = cholesky_upper(gram_re, gram_im)
    fac_re, fac_im = joined((fac_re, fac_im), "space", combine_factors)
    inv_re, inv_im = invert_upper(fac_re, fac_im)
    mode_blocks = apply_inverse(owned_spec, inv_re, inv_im)
    upper_factor = jnp.transpose(jnp.stack([fac_re, fac_im], 0), (3, 0, 1, 2))
    return (mode_blocks, upper_factor)


def solution(mesh):
    placed = (P("tm", None, "space"), P("space"))
    return jax.shard_map(
        body,
        mesh=mesh,
        in_specs=placed,
        out_specs=(P(None, "tm", None, "space"), P("tm", None, None, None)),
        check_vma=False,
    )
```

profile of v0, /device:TPU:1, one launch (start us, length us, event | category | flops | bytes accessed | tf_op | source)
XLA Modules:
  0.0 409.4 jit_solution(2311349032449920619)
XLA Ops:
  0.7 5.7 %reduce_sum.9 = f32[2,4096]{1,0:T(2,128)S(1)} reduce(f32[256,2,4096]{2,1,0:T(2,128)} %param.4, f32[]{:T(128)} %constant.93.clone.1), dimensions={0}, to_apply=%region_0.0 | reduce | flops 2088960 | bytes 8421380 | tf_op jit(solution)/shard_map/reduce_sum | solution.py:136
  6.4 28.6 %psum.7 = f32[2,4096]{1,0:T(2,128)S(1)} all-reduce(f32[2,4096]{1,0:T(2,128)S(1)} %reduce_sum.9), channel_id=1, replica_groups=mesh['tm'=8,'space'=32] {'tm'}, use_global_device_ids=true, to_apply=%region_1.0 | all-reduce | flops 8192 | bytes 65536 | tf_op jit(solution)/shard_map/psum | solution.py:137
  35.0 6.4 %subtract_bitcast_fusion = f32[1,256,2,4096]{3,2,1,0:T(2,128)S(1)} fusion(f32[256,2,4096]{2,1,0:T(2,128)} %param.4, f32[2,4096]{1,0:T(2,128)S(1)} %broadcast_multiply_fusion.1), kind=kLoop, calls=%fused_computation.359 | loop fusion | flops 2097152 | bytes 16809984 | tf_op jit(solution)/shard_map/sub | solution.py:138
  41.4 9.9 %fusion.731 = (f32[1,256,1,4096]{3,2,1,0:T(1,128)S(1)}, f32[1,256,1,4096]{3,2,1,0:T(1,128)S(1)}) fusion(f32[1,256,2,4096]{3,2,1,0:T(2,128)S(1)} %subtract_bitcast_fusion), kind=kLoop, calls=%fused_computation.1509 | loop fusion | bytes 16777216 | tf_op jit(solution)/shard_map/slice | solution.py:35
  51.2 5.3 %fusion.106 = f32[4096,64]{0,1:T(8,128)S(1)} fusion(f32[1,256,1,4096]{3,2,1,0:T(1,128)S(1)} %get-tuple-element.612, f32[256]{0:T(256)S(1)} %multiply_subtract_fusion.4), kind=kOutput, calls=%fused_computation.372 | convolution fusion | flops 805552128 | bytes 5243904 | tf_op jit(solution)/shard_map/kj,bjp->bkp/dot_general | solution.py:35
  56.6 5.3 %fusion.102 = f32[4096,64]{0,1:T(8,128)S(1)} fusion(f32[1,256,1,4096]{3,2,1,0:T(1,128)S(1)} %get-tuple-element.613, f32[256]{0:T(256)S(1)} %multiply_subtract_fusion.4), kind=kOutput, calls=%fused_computation.368 | convolution fusion | flops 805552128 | bytes 5243904 | tf_op jit(solution)/shard_map/kj,bjp->bkp/dot_general | solution.py:38
  61.9 5.5 %fusion.99 = f32[1,64,1,4096]{3,1,2,0:T(8,128)S(1)} fusion(f32[4096,64]{0,1:T(8,128)S(1)} %fusion.106, f32[1,256,1,4096]{3,2,1,0:T(1,128)S(1)} %get-tuple-element.613, f32[256]{0:T(256)S(1)} %multiply_subtract_fusion.4), kind=kOutput, calls=%fused_computation.365 | convolution fusion | flops 805814272 | bytes 6292480 | tf_op jit(solution)/shard_map/kj,bjp->bkp/dot_general | solution.py:35
  67.4 5.3 %fusion.98 = f32[1,64,1,4096]{3,1,2,0:T(8,128)S(1)} fusion(f32[4096,64]{0,1:T(8,128)S(1)} %fusion.102, f32[1,256,1,4096]{3,2,1,0:T(1,128)S(1)} %get-tuple-element.612, f32[256]{0:T(256)S(1)} %multiply_subtract_fusion.4), kind=kOutput, calls=%fused_computation.363 | convolution fusion | flops 805814272 | bytes 6292480 | tf_op jit(solution)/shard_map/kj,bjp->bkp/dot_general | solution.py:38
  72.9 2.9 copy.145
  75.8 3.9 all-to-all-start
  79.8 19.2 %all-to-all-done = f32[1,64,2,4096]{3,2,0,1:T(2,128)S(1)} async-done(((f32[1,64,2,4096]{3,2,0,1:T(2,128)}), f32[1,64,2,4096]{3,2,0,1:T(2,128)S(1)}, u32[]{:S(2)}, u32[]{:S(2)}) %all-to-all-start) | async-done | bytes 2097184 | tf_op jit(solution)/shard_map/all_to_all | solution.py:142
  99.0 1.2 copy.208
  100.3 1.3 fusion.732
  101.5 2.2 fusion.115
  103.8 2.1 fusion.113
  106.8 2.2 fusion.114
  109.0 2.2 fusion.112
  113.7 60.0 %all-gather.1 = f32[256,8,8]{2,1,0:T(8,128)S(1)} all-gather(f32[8,8,8]{2,1,0:T(8,128)S(1)} %copy.157), channel_id=3, replica_groups=mesh['tm'=8,'space'=32] {'space'}, dimensions={0}, use_global_device_ids=true | all-gather | bytes 67584 | tf_op jit(solution)/shard_map/all_gather | solution.py:14
  173.9 43.3 %all-gather = f32[256,8,8]{2,1,0:T(8,128)S(1)} all-gather(f32[8,8,8]{2,1,0:T(8,128)S(1)} %constant_dynamic-update-slice_fusion.16), channel_id=2, replica_groups=mesh['tm'=8,'space'=32] {'space'}, dimensions={0}, use_global_device_ids=true | all-gather | bytes 67584 | tf_op jit(solution)/shard_map/all_gather | solution.py:14
  217.3 1.0 copy-done
  218.2 180.1 %while.17 = (s32[]{:T(128)}, f32[8,8,8]{2,1,0:T(8,128)S(1)}, f32[8,8,8]{2,1,0:T(8,128)S(1)}, f32[32,8,8,8]{3,2,1,0:T(8,128)}, f32[32,8,8,8]{3,2,1,0:T(8,128)S(1)...) while((s32[]{:T(128)}, f32[8,8,8]{2,1,0:T(8,128)S(1)}, f32[8,8,8]{2,1,0:T(8,128)S(1)}, ...), condition=%wide.region_3.4_spmd, body=%wide.region_2.3_spmd.sunk | while | flops 402373 | bytes 223575 | solution.py:19
  218.5 0.8 constant_dynamic-slice_fusion.3
  224.3 0.8 constant_dynamic-slice_fusion.3
  230.1 0.8 constant_dynamic-slice_fusion.3
  235.9 0.8 constant_dynamic-slice_fusion.3
  270.7 0.8 constant_dynamic-slice_fusion.3
  380.9 0.8 constant_dynamic-slice_fusion.3
  400.4 1.0 fusion.117
  402.4 1.0 fusion.116
  403.4 1.0 fusion.100
  404.4 1.0 fusion.101
  405.6 2.9 copy.178
  (1923 shorter events, 173.9 us)
Async XLA Ops:
  75.8 4.0 copy-start.1
  75.8 23.2 %all-to-all-start = ((f32[1,64,2,4096]{3,2,0,1:T(2,128)}), f32[1,64,2,4096]{3,2,0,1:T(2,128)S(1)}, u32[]{:S(2)}, u32[]{:S(2)}) async-start(f32[1,64,2,4096]{3,2,0,1:T(2,128)} %copy.145), calls=%async_computation | async-start | bytes 4194304 | tf_op jit(solution)/shard_map/all_to_all | solution.py:142
  217.3 1.0 copy-start
where the time goes:
time: 415 us; the launch traced here: 409 us
  blocking collectives  132 us (32%)
  local copies, waits for them, and re-layouts  126 us (30%)
  matrix products  89.7 us (22%)
  other arithmetic  28.5 us (7%)
  waiting for transfers between devices  19.2 us (5%)
  loops' own time  9.22 us (2%)
    all_gather x2, blocking collectives, joined(): gathered = jax.tree.map(lambda a: lax.all_gather(a, axis), part)  103 us
    dynamic_slice x95, local copies, waits for them, and re-layouts, take(): lax.dynamic_index_in_dim(a, source, 0, False)  28.8 us
    psum x1, blocking collectives, body(): time_mean = lax.psum(block_total, 'tm') / (NB * NFFT)  28.6 us
    slice x64, local copies, waits for them, and re-layouts, cholesky_upper(): acc_im = gram_im[j, i]  23.9 us
    all_to_all x1, waiting for transfers between devices, body(): lax.all_to_all(spectra, 'tm', split_axis=1, concat_axis=0, tiled=True)  19.2 us
    slice x32, local copies, waits for them, and re-layouts, cholesky_upper(): pivot_sq = gram_re[j, j]  16.4 us
    dot_general x62, matrix products, factor_gram(): jnp.einsum('kaf,kbf->abf', fac_re, fac_im, precision=highest)  14.2 us
    slice x32, local copies, waits for them, and re-layouts, cholesky_upper(): acc_re = gram_re[j, i]  14 us
  transfers between devices with their start and end apart: 1, of which 1 were waited for; matrix products, arithmetic and copies ran while one was open for 0% of the time, Pallas kernels for 0%

commit v1 on v0

--- a/solution.py
+++ b/solution.py
@@ -10,17 +10,6 @@
 KF = 64
 
 
-def joined(part, axis, combine):
-    gathered = jax.tree.map(lambda a: lax.all_gather(a, axis), part)
-
-    def take(source):
-        return jax.tree.map(lambda a: lax.dynamic_index_in_dim(a, source, 0, False), gathered)
-
-    return lax.fori_loop(
-        1, lax.axis_size(axis), lambda source, state: combine(state, take(source)), take(0)
-    )
-
-
 def dft_tables():
     column = jnp.arange(NFFT, dtype=jnp.int32)
     freqs = jnp.arange(KF, dtype=jnp.int32)
@@ -31,7 +20,7 @@
 
 
 def transform(centered, cos_tab, sin_tab):
-    highest = lax.Precision.HIGHEST
+    highest = lax.Precision.HIGH
     spec_re = jnp.einsum("kj,bjp->bkp", cos_tab, centered[:, :, 0], precision=highest) + jnp.einsum(
         "kj,bjp->bkp", sin_tab, centered[:, :, 1], precision=highest
     )
@@ -42,7 +31,7 @@
 
 
 def local_gram(spectra, scaled):
-    highest = lax.Precision.HIGHEST
+    highest = lax.Precision.HIGH
     weighted = spectra * scaled
     gram_re = jnp.einsum(
         "afp,bfp->abf", weighted[:, :, 0], spectra[:, :, 0], precision=highest
@@ -50,17 +39,6 @@
     gram_im = jnp.einsum(
         "afp,bfp->abf", weighted[:, :, 0], spectra[:, :, 1], precision=highest
     ) - jnp.einsum("afp,bfp->abf", weighted[:, :, 1], spectra[:, :, 0], precision=highest)
-    return (gram_re, gram_im)
-
-
-def factor_gram(fac_re, fac_im):
-    highest = lax.Precision.HIGHEST
-    gram_re = jnp.einsum("kaf,kbf->abf", fac_re, fac_re, precision=highest) + jnp.einsum(
-        "kaf,kbf->abf", fac_im, fac_im, precision=highest
-    )
-    gram_im = jnp.einsum("kaf,kbf->abf", fac_re, fac_im, precision=highest) - jnp.einsum(
-        "kaf,kbf->abf", fac_im, fac_re, precision=highest
-    )
     return (gram_re, gram_im)
 
 
@@ -94,12 +72,6 @@
     return (stack_rows(upper_re), stack_rows(upper_im))
 
 
-def combine_factors(left_pair, right_pair):
-    left_re, left_im = factor_gram(left_pair[0], left_pair[1])
-    right_re, right_im = factor_gram(right_pair[0], right_pair[1])
-    return cholesky_upper(left_re + right_re, left_im + right_im)
-
-
 def invert_upper(upper_re, upper_im):
     size_n = upper_re.shape[0]
     zero_row = jnp.zeros_like(upper_re[0, 0])
@@ -119,7 +91,7 @@
 
 
 def apply_inverse(spectra, inv_re, inv_im):
-    highest = lax.Precision.HIGHEST
+    highest = lax.Precision.HIGH
     mode_re = jnp.einsum("afp,abf->bfp", spectra[:, :, 0], inv_re, precision=highest) - jnp.einsum(
         "afp,abf->bfp", spectra[:, :, 1], inv_im, precision=highest
     )
@@ -140,9 +112,9 @@
     spectra = transform(centered, cos_tab, sin_tab)
     scaled = quad_weights / point_total
     owned_spec = lax.all_to_all(spectra, "tm", split_axis=1, concat_axis=0, tiled=True)
-    gram_re, gram_im = local_gram(owned_spec, scaled)
+    share = jnp.stack(local_gram(owned_spec, scaled), 0)
+    gram_re, gram_im = lax.psum(share, "space")
     fac_re, fac_im = cholesky_upper(gram_re, gram_im)
-    fac_re, fac_im = joined((fac_re, fac_im), "space", combine_factors)
     inv_re, inv_im = invert_upper(fac_re, fac_im)
     mode_blocks = apply_inverse(owned_spec, inv_re, inv_im)
     upper_factor = jnp.transpose(jnp.stack([fac_re, fac_im], 0), (3, 0, 1, 2))

time: 415 us -> 271 us (0.65)
  local copies, waits for them, and re-layouts: 126 us -> 33.9 us
  matrix products: 89.7 us -> 21.3 us
  blocking collectives: 132 us -> 171 us
  other arithmetic: 28.5 us -> 16.7 us
  loops' own time: 9.22 us -> 0 us
    psum x0 -> x1, blocking collectives: none -> 142 us  [body(): gram_re, gram_im = lax.psum(share, 'space')]
    all_gather x2 -> x0, blocking collectives: 103 us -> none  [joined(): gathered = jax.tree.map(lambda a: lax.all_gather(a, axis), part)]
    dot_general x248 -> x0, matrix products: 55.6 us -> none  [the longest x62 14.2 us: factor_gram(): jnp.einsum('kaf,kbf->abf', fac_re, fac_im, precision=highest)]
    dynamic_slice x95 -> x0, local copies, waits for them, and re-layouts: 28.8 us -> none  [take(): lax.dynamic_index_in_dim(a, source, 0, False)]
    slice x64 -> x2, local copies, waits for them, and re-layouts: 23.9 us -> 0.74 us  [cholesky_upper(): acc_im = gram_im[j, i]]
    slice x32 -> x1, local copies, waits for them, and re-layouts: 16.4 us -> 0.51 us  [cholesky_upper(): pivot_sq = gram_re[j, j]]
    slice x32 -> x1, local copies, waits for them, and re-layouts: 14 us -> 0.44 us  [cholesky_upper(): acc_re = gram_re[j, i]]
    another operation x221 -> x5, local copies, waits for them, and re-layouts: 10.7 us -> 0.02 us
where the time goes in v1:
time: 271 us; the launch traced here: 267 us
  blocking collectives  171 us (63%)
  local copies, waits for them, and re-layouts  33.9 us (13%)
  matrix products  21.3 us (8%)
  waiting for transfers between devices  19.2 us (7%)
  other arithmetic  16.7 us (6%)
  starting transfers between devices  3.74 us (1%)
    psum x1, blocking collectives, body(): gram_re, gram_im = lax.psum(share, 'space')  142 us
    psum x1, blocking collectives, body(): time_mean = lax.psum(block_total, 'tm') / (NB * NFFT)  28.6 us
    all_to_all x1, waiting for transfers between devices, body(): lax.all_to_all(spectra, 'tm', split_axis=1, concat_axis=0, tiled=True)  19.2 us
    another operation x56, local copies, waits for them, and re-layouts, stack_rows(): return jnp.stack([jnp.stack(entries, 0) for entries in table], 0)  14.8 us
    slice x1, local copies, waits for them, and re-layouts, transform(): centered[:, :, 0]  9.6 us
    sub x1, other arithmetic, body(): centered = snapshots.reshape(blocks_dev, NFFT, 2, cell_count) - time_mean  6.37 us
    reduce_sum x1, other arithmetic, body(): block_total = jnp.sum(snapshots, axis=0)  5.67 us
  transfers between devices with their start and end apart: 1, of which 1 were waited for; matrix products, arithmetic and copies ran while one was open for 0% of the time, Pallas kernels for 0%

profile of v1, /device:TPU:1, one launch (start us, length us, event | category | flops | bytes accessed | tf_op | source)
XLA Modules:
  0.0 267.0 jit_solution(9443683229390016158)
XLA Ops:
  0.7 5.7 %reduce_sum.9 = f32[2,4096]{1,0:T(2,128)S(1)} reduce(f32[256,2,4096]{2,1,0:T(2,128)} %param.2, f32[]{:T(128)} %constant.15.clone.1), dimensions={0}, to_apply=%region_0.0 | reduce | flops 2088960 | bytes 8421380 | tf_op jit(solution)/shard_map/reduce_sum | solution.py:108
  6.4 28.6 %psum.14 = f32[2,4096]{1,0:T(2,128)S(1)} all-reduce(f32[2,4096]{1,0:T(2,128)S(1)} %reduce_sum.9), channel_id=1, replica_groups=mesh['tm'=8,'space'=32] {'tm'}, use_global_device_ids=true, to_apply=%region_1.0 | all-reduce | flops 8192 | bytes 65536 | tf_op jit(solution)/shard_map/psum | solution.py:109
  35.0 6.4 %subtract_bitcast_fusion = f32[1,256,2,4096]{3,2,1,0:T(2,128)S(1)} fusion(f32[256,2,4096]{2,1,0:T(2,128)} %param.2, f32[2,4096]{1,0:T(2,128)S(1)} %broadcast_multiply_fusion.1), kind=kLoop, calls=%fused_computation | loop fusion | flops 2097152 | bytes 16809984 | tf_op jit(solution)/shard_map/sub | solution.py:110
  41.4 9.6 %fusion.606 = (f32[1,256,1,4096]{3,2,1,0:T(1,128)S(1)}, f32[1,256,1,4096]{3,2,1,0:T(1,128)S(1)}) fusion(f32[1,256,2,4096]{3,2,1,0:T(2,128)S(1)} %subtract_bitcast_fusion), kind=kLoop, calls=%fused_computation.1144 | loop fusion | bytes 16777216 | tf_op jit(solution)/shard_map/slice | solution.py:24
  51.0 3.6 %fusion.4 = f32[4096,64]{0,1:T(8,128)S(1)} fusion(f32[1,256,1,4096]{3,2,1,0:T(1,128)S(1)} %get-tuple-element.210, f32[256]{0:T(256)S(1)} %multiply_subtract_fusion), kind=kOutput, calls=%fused_computation.9 | convolution fusion | flops 402898944 | bytes 5243904 | tf_op jit(solution)/shard_map/kj,bjp->bkp/dot_general | solution.py:27
  54.5 3.6 %fusion.8 = f32[4096,64]{0,1:T(8,128)S(1)} fusion(f32[1,256,1,4096]{3,2,1,0:T(1,128)S(1)} %get-tuple-element.209, f32[256]{0:T(256)S(1)} %multiply_subtract_fusion), kind=kOutput, calls=%fused_computation.13 | convolution fusion | flops 402898944 | bytes 5243904 | tf_op jit(solution)/shard_map/kj,bjp->bkp/dot_general | solution.py:24
  58.1 3.6 %fusion = f32[1,64,1,4096]{3,1,2,0:T(8,128)S(1)} fusion(f32[4096,64]{0,1:T(8,128)S(1)} %fusion.4, f32[1,256,1,4096]{3,2,1,0:T(1,128)S(1)} %get-tuple-element.209, f32[256]{0:T(256)S(1)} %multiply_subtract_fusion), kind=kOutput, calls=%fused_computation.4 | convolution fusion | flops 403161088 | bytes 6292480 | tf_op jit(solution)/shard_map/kj,bjp->bkp/dot_general | solution.py:27
  61.6 3.8 %fusion.1 = f32[1,64,1,4096]{3,1,2,0:T(8,128)S(1)} fusion(f32[4096,64]{0,1:T(8,128)S(1)} %fusion.8, f32[1,256,1,4096]{3,2,1,0:T(1,128)S(1)} %get-tuple-element.210, f32[256]{0:T(256)S(1)} %multiply_subtract_fusion), kind=kOutput, calls=%fused_computation.6 | convolution fusion | flops 403161088 | bytes 6292480 | tf_op jit(solution)/shard_map/kj,bjp->bkp/dot_general | solution.py:24
  65.6 2.9 %copy.107 = f32[1,64,2,4096]{3,2,0,1:T(2,128)} copy(f32[1,64,2,4096]{3,1,2,0:T(8,128)S(1)} %pad_maximum_fusion) | data formatting | bytes 4194304 | tf_op jit(solution)/shard_map/stack | solution.py:30
  68.5 3.7 %all-to-all-start = ((f32[1,64,2,4096]{3,2,0,1:T(2,128)}), f32[1,64,2,4096]{3,2,0,1:T(2,128)S(1)}, u32[]{:S(2)}, u32[]{:S(2)}) async-start(f32[1,64,2,4096]{3,2,0,1:T(2,128)} %copy.107), calls=%async_computation | async-start | bytes 4194304 | tf_op jit(solution)/shard_map/all_to_all | solution.py:114
  72.3 19.2 %all-to-all-done = f32[1,64,2,4096]{3,2,0,1:T(2,128)S(1)} async-done(((f32[1,64,2,4096]{3,2,0,1:T(2,128)}), f32[1,64,2,4096]{3,2,0,1:T(2,128)S(1)}, u32[]{:S(2)}, u32[]{:S(2)}) %all-to-all-start) | async-done | bytes 2097184 | tf_op jit(solution)/shard_map/all_to_all | solution.py:114
  91.5 1.2 copy.165
  92.7 1.3 fusion.607
  94.0 1.2 fusion.16
  95.2 1.2 fusion.17
  96.4 1.2 fusion.14
  97.5 1.0 fusion.15
  98.6 142.5 %psum.15 = f32[2,8,8,8]{1,2,3,0:T(8,128)S(1)} all-reduce(f32[2,8,8,8]{1,2,3,0:T(8,128)S(1)} %pad_maximum_fusion.2), channel_id=1, replica_groups=mesh['tm'=8,'space'=32] {'space'}, use_global_device_ids=true, to_apply=%region_2.3 | all-reduce | flops 1024 | bytes 8192 | tf_op jit(solution)/shard_map/psum | solution.py:116
  247.5 0.7 copy.129
  248.3 0.7 copy.130
  249.0 0.7 copy.131
  249.7 0.7 copy.132
  251.1 0.7 copy.134
  254.2 0.7 copy.112
  255.0 0.7 copy.113
  255.7 0.7 copy.114
  256.4 0.7 copy.115
  257.9 0.7 copy.117
  258.6 0.7 copy.118
  259.3 0.7 copy.119
  260.0 1.0 stack.408
  263.0 2.9 %copy.142 = f32[8,8,2,4096]{3,2,1,0:T(2,128)} copy(f32[8,8,2,4096]{3,0,1,2:T(8,128)S(1)} %pad_maximum_fusion.1) | data formatting | bytes 4194304
  (103 shorter events, 13.2 us)
Async XLA Ops:
  68.5 3.7 %copy-start.6 = (f32[4096]{0:T(1024)S(1)}, f32[4096]{0:T(1024)}, u32[]{:S(2)}) copy-start(f32[4096]{0:T(1024)} %param.3) | copy-start | bytes 49156
  68.5 23.0 %all-to-all-start = ((f32[1,64,2,4096]{3,2,0,1:T(2,128)}), f32[1,64,2,4096]{3,2,0,1:T(2,128)S(1)}, u32[]{:S(2)}, u32[]{:S(2)}) async-start(f32[1,64,2,4096]{3,2,0,1:T(2,128)} %copy.107), calls=%async_computation | async-start | bytes 4194304 | tf_op jit(solution)/shard_map/all_to_all | solution.py:114
  247.4 6.1 %copy-start.7 = (f32[1,8]{1,0:T(1,128)S(1)}, f32[1,8]{1,0:T(1,128)}, u32[]{:S(2)}) copy-start(f32[1,8]{1,0:T(1,128)} %get-tuple-element.111) | copy-start | bytes 100
  263.0 3.1 %copy-start = (f32[1,8,8]{0,1,2:T(8,128)S(1)}, f32[1,8,8]{0,1,2:T(8,128)}, u32[]{:S(2)}) copy-start(f32[1,8,8]{0,1,2:T(8,128)} %copy.129) | copy-start | bytes 772
  263.0 3.1 %copy-start.1 = (f32[1,8,8]{0,1,2:T(8,128)S(1)}, f32[1,8,8]{0,1,2:T(8,128)}, u32[]{:S(2)}) copy-start(f32[1,8,8]{0,1,2:T(8,128)} %copy.130) | copy-start | bytes 772
  263.0 3.1 %copy-start.2 = (f32[1,8,8]{0,1,2:T(8,128)S(1)}, f32[1,8,8]{0,1,2:T(8,128)}, u32[]{:S(2)}) copy-start(f32[1,8,8]{0,1,2:T(8,128)} %copy.131) | copy-start | bytes 772
  263.0 3.1 %copy-start.3 = (f32[1,8,8]{0,1,2:T(8,128)S(1)}, f32[1,8,8]{0,1,2:T(8,128)}, u32[]{:S(2)}) copy-start(f32[1,8,8]{0,1,2:T(8,128)} %copy.132) | copy-start | bytes 772
  263.0 3.1 %copy-start.4 = (f32[1,8,8]{0,1,2:T(8,128)S(1)}, f32[1,8,8]{0,1,2:T(8,128)}, u32[]{:S(2)}) copy-start(f32[1,8,8]{0,1,2:T(8,128)} %copy.133) | copy-start | bytes 772
  263.0 3.1 %copy-start.5 = (f32[1,8,8]{0,1,2:T(8,128)S(1)}, f32[1,8,8]{0,1,2:T(8,128)}, u32[]{:S(2)}) copy-start(f32[1,8,8]{0,1,2:T(8,128)} %copy.134) | copy-start | bytes 772

commit v2 on v1

v2 whole, which is shorter than its diff:
```python
import functools
import math

import jax
import jax.numpy as jnp
import ml_dtypes
import numpy as np
from jax import lax
from jax.experimental import pallas as pl
from jax.experimental.pallas import tpu as pltpu
from jax.sharding import PartitionSpec as P

NB = 8
NFFT = 256
KF = 64
LANES = 128
EARLY = 2
SPLIT = 6
MESH = pl.DeviceIdType.MESH

PAIRS_RE = [(a, b) for a in range(NB) for b in range(a, NB)]
PAIRS_IM = [(a, b) for a in range(NB) for b in range(a + 1, NB)]
SLOT_RE = {pair: i for i, pair in enumerate(PAIRS_RE)}
SLOT_IM = {pair: len(PAIRS_RE) + i for i, pair in enumerate(PAIRS_IM)}
SLOTS = len(PAIRS_RE) + len(PAIRS_IM)


def tables():
    j = np.arange(NFFT)
    k = np.arange(KF)
    window = 0.54 - 0.46 * np.cos(2.0 * math.pi * j / NFFT)
    angles = 2.0 * math.pi * (k[:, None] * j[None, :] % NFFT) / NFFT
    cos_tab = window * np.cos(angles)
    sin_tab = window * np.sin(angles)
    full = np.zeros((2, KF, NFFT, 2))
    full[0, :, :, 0] = cos_tab
    full[0, :, :, 1] = sin_tab
    full[1, :, :, 0] = -sin_tab
    full[1, :, :, 1] = cos_tab
    full = full.reshape(2 * KF, 2 * NFFT).astype(np.float32)
    high = full.astype(ml_dtypes.bfloat16)
    low = (full - high.astype(np.float32)).astype(ml_dtypes.bfloat16)
    ones = np.ones((1, LANES))
    window_re = (cos_tab.sum(1)[:, None] * ones).astype(np.float32)
    window_im = (-sin_tab.sum(1)[:, None] * ones).astype(np.float32)
    return np.concatenate([high, low], 0), np.stack([window_re, window_im], 0)


def turned(z, even):
    return jnp.where(even, pltpu.roll(z, 7, 0), -pltpu.roll(z, 1, 0))


def cholesky(gram_re, gram_im):
    up_re, up_im, diag_inv = {}, {}, {}
    for j in range(NB):
        pivot = gram_re[j, j]
        for k in range(j):
            pivot = pivot - (up_re[k, j] * up_re[k, j] + up_im[k, j] * up_im[k, j])
        inv = lax.rsqrt(pivot)
        inv = inv * (1.5 - 0.5 * ((pivot * inv) * inv))
        diag_inv[j] = inv
        up_re[j, j] = pivot * inv
        for i in range(j + 1, NB):
            acc_re, acc_im = gram_re[j, i], gram_im[j, i]
            for k in range(j):
                acc_re = acc_re - (up_re[k, j] * up_re[k, i] + up_im[k, j] * up_im[k, i])
                acc_im = acc_im - (up_re[k, j] * up_im[k, i] - up_im[k, j] * up_re[k, i])
            up_re[j, i] = acc_re * inv
            up_im[j, i] = acc_im * inv
    inv_re, inv_im = {}, {}
    for j in range(NB):
        inv_re[j, j] = diag_inv[j]
        for i in range(j - 1, -1, -1):
            acc_re = up_re[i, j] * inv_re[j, j]
            acc_im = up_im[i, j] * inv_re[j, j]
            for k in range(i + 1, j):
                acc_re = acc_re + up_re[i, k] * inv_re[k, j] - up_im[i, k] * inv_im[k, j]
                acc_im = acc_im + up_re[i, k] * inv_im[k, j] + up_im[i, k] * inv_re[k, j]
            inv_re[i, j] = -acc_re * diag_inv[i]
            inv_im[i, j] = -acc_im * diag_inv[i]
    return up_re, up_im, inv_re, inv_im


def kernel(
    point_total, x_hbm, w_hbm, tab_hbm, win_hbm, modes_hbm, factor_ref,
    xs, tab, win, wgt, wgt2, spec, sums, sums_in, mean_part, mean, recv, turn, prod, acc, inverse, modes,
    share, core_in, half, space_in,
    x_sem, in_sem, send_sem, recv_sem, sums_sem, mean_sem, small_sem, core_sem, space_sem, out_sem,
):
    tm = lax.axis_index("tm")
    sp = lax.axis_index("space")
    points = xs.shape[0]
    rows = 2 * points
    steps = points // 4
    per = KF // NB

    z_hi, y, core = lax.div(sp, 8), lax.rem(lax.div(sp, 2), 4), lax.rem(sp, 2)
    mates = [lax.rem(tm + d, NB) for d in range(1, NB)]
    core_peer = z_hi * 8 + y * 2 + (1 - core)
    space_peers = [
        lax.rem(z_hi + dz, 4) * 8 + lax.rem(y + dy, 4) * 2 + core
        for dz in range(4)
        for dy in range(4)
        if (dz, dy) != (0, 0)
    ]

    def x_copy(pt):
        return pltpu.make_async_copy(x_hbm.at[:, pt], xs.at[pt], x_sem.at[pt // 4])

    tab_copy = pltpu.make_async_copy(tab_hbm, tab, in_sem.at[0])
    win_copy = pltpu.make_async_copy(win_hbm, win, in_sem.at[1])
    wgt_copy = pltpu.make_async_copy(w_hbm, wgt, in_sem.at[2])
    for pt in range(4):
        x_copy(pt).start()
    tab_copy.start()
    win_copy.start()
    for pt in range(4, points):
        x_copy(pt).start()
    wgt_copy.start()

    barrier = pltpu.get_barrier_semaphore()
    for mate in mates:
        pl.semaphore_signal(barrier, 1, device_id=(mate, sp), device_id_type=MESH)
    for peer in [core_peer, *space_peers]:
        pl.semaphore_signal(barrier, 1, device_id=(tm, peer), device_id_type=MESH)

    row8 = lax.broadcasted_iota(jnp.int32, (8, LANES), 0)
    lane8 = lax.broadcasted_iota(jnp.int32, (8, LANES), 1)
    even = lax.rem(row8, 2) == 0
    spec_rows = spec.reshape(KF * rows, LANES)

    def remote(src, dst, recv_at, mate=None, peer=None, sent=None):
        return pltpu.make_async_remote_copy(
            src, dst, send_sem if sent is None else sent, recv_at,
            device_id=(tm if mate is None else mate, sp if peer is None else peer), device_id_type=MESH,
        )

    def transform_step(q):
        pltpu.make_async_copy(xs.at[pl.ds(4 * q, 4)], xs.at[pl.ds(4 * q, 4)], x_sem.at[q]).wait()
        highs, lows, bases = [], [], []
        totals = None
        for i in range(4):
            v = xs.at[4 * q + i].reshape(2 * NFFT, LANES)[...]
            base = v[0:8]
            base = base + pltpu.roll(base, 4, 0)
            base = (base + pltpu.roll(base, 2, 0)) * 0.25
            d = v.reshape(NFFT // 4, 8, LANES) - base[None]
            total = jnp.sum(d, axis=0)
            total = total + pltpu.roll(total, 4, 0)
            total = total + pltpu.roll(total, 2, 0) + base * NFFT
            totals = total if i == 0 else jnp.where(lax.div(row8, 2) == i, total, totals)
            d = d.reshape(2 * NFFT, LANES)
            high = d.astype(jnp.bfloat16)
            highs.append(high)
            lows.append((d - high.astype(jnp.float32)).astype(jnp.bfloat16))
            bases.append(base)
        both = jnp.dot(tab[...], jnp.concatenate(highs, 1), preferred_element_type=jnp.float32)
        rest = jnp.dot(tab[: 2 * KF], jnp.concatenate(lows, 1), preferred_element_type=jnp.float32)
        out = both[: 2 * KF] + both[2 * KF :] + rest
        for i in range(4):
            at = slice(i * LANES, (i + 1) * LANES)
            base_re, base_im = bases[i][0:1], bases[i][1:2]
            spec_rows[pl.ds(8 * q + 2 * i, KF, stride=rows), :] = (
                out[:KF, at] + (win[0] * base_re - win[1] * base_im)
            )
            spec_rows[pl.ds(8 * q + 2 * i + 1, KF, stride=rows), :] = (
                out[KF:, at] + (win[0] * base_im + win[1] * base_re)
            )
        sums[pl.ds(pl.multiple_of(8 * q, 8), 8), :] = totals

    def early_sends(q):
        at = pl.ds(pl.multiple_of(8 * q, 8), 8)
        for mate in mates:
            remote(
                spec.at[mate, pl.ds(0, EARLY), at], recv.at[pl.ds(0, EARLY), tm, at], recv_sem.at[0], mate=mate
            ).start()

    tab_copy.wait()
    win_copy.wait()
    transform_step(0)
    pl.semaphore_wait(barrier, len(mates) + 1 + len(space_peers))
    early_sends(0)

    @pl.loop(1, steps)
    def _(q):
        transform_step(q)
        early_sends(q)

    pltpu.make_async_copy(spec.at[tm, pl.ds(0, EARLY)], recv.at[pl.ds(0, EARLY), tm], recv_sem.at[0]).start()
    for mate in mates:
        remote(
            sums.at[pl.ds(pl.multiple_of(8 * mate, 8), 8)], sums_in.at[tm], sums_sem, mate=mate, sent=small_sem.at[0]
        ).start()
    pltpu.make_async_copy(sums.at[pl.ds(pl.multiple_of(8 * tm, 8), 8)], sums_in.at[tm], sums_sem).start()
    for f in range(EARLY, per):
        for mate in mates:
            remote(spec.at[mate, f], recv.at[f, tm], recv_sem.at[f], mate=mate).start()
        pltpu.make_async_copy(spec.at[tm, f], recv.at[f, tm], recv_sem.at[f]).start()

    pltpu.make_async_copy(sums_in, sums_in, sums_sem).wait()
    part = sums_in[0]
    for a in range(1, NB):
        part = part + sums_in[a]
    mean_part[...] = part * (1.0 / (NB * NFFT))
    for mate in mates:
        remote(mean_part, mean.at[tm], mean_sem, mate=mate, sent=small_sem.at[1]).start()
    pltpu.make_async_copy(mean_part, mean.at[tm], mean_sem).start()
    wgt_copy.wait()
    scaled = wgt[...] / point_total
    wgt2[pl.ds(0, points, stride=2), :] = scaled
    wgt2[pl.ds(1, points, stride=2), :] = scaled
    pltpu.make_async_copy(mean, mean, mean_sem).wait()

    groups = rows // 8

    def gram_step(f, total):
        win_re = jnp.broadcast_to(win[0, pl.ds(per * tm + f, 1), :], (8, LANES))
        win_im = jnp.broadcast_to(win[1, pl.ds(per * tm + f, 1), :], (8, LANES))
        for g in range(groups):
            at = pl.ds(8 * g, 8)
            m = mean[g]
            shift = win_re * m - win_im * turned(m, even)
            weight = wgt2[at, :]
            for a in range(NB):
                z = recv[f, a, at, :] - shift
                recv[f, a, at, :] = z
                turn[f, a, at, :] = turned(z, even)
                prod[a, at, :] = z * weight
        for a in range(NB):
            sums_re = {}
            sums_im = {}
            for g in range(groups):
                at = pl.ds(8 * g, 8)
                p = prod[a, at, :]
                for b in range(a, NB):
                    term = p * recv[f, b, at, :]
                    sums_re[b] = term if g == 0 else sums_re[b] + term
                    if b > a:
                        term = p * turn[f, b, at, :]
                        sums_im[b] = term if g == 0 else sums_im[b] + term
            for b in range(a, NB):
                acc[pl.ds(8 * SLOT_RE[a, b], 8), :] = sums_re[b]
                if b > a:
                    acc[pl.ds(8 * SLOT_IM[a, b], 8), :] = sums_im[b]
        folded = acc[pl.ds(0, SLOTS, stride=8), :]
        for s in range(1, 8):
            folded = folded + acc[pl.ds(s, SLOTS, stride=8), :]
        folded = jnp.concatenate([folded, jnp.zeros((LANES - SLOTS, LANES), jnp.float32)], 0)
        line = lax.dot_general(
            jnp.ones((8, LANES), jnp.float32), folded, (((1,), (1,)), ((), ())),
            precision=lax.Precision.HIGHEST, preferred_element_type=jnp.float32,
        )
        return jnp.where(row8 == f, line, total)

    def waited_gram_step(f, total):
        pltpu.make_async_copy(recv.at[f], recv.at[f], recv_sem.at[f]).wait()
        return gram_step(f, total)

    def core_start(n, total):
        share[n] = total
        remote(share.at[n], core_in.at[n], core_sem.at[n, 0], peer=core_peer, sent=core_sem.at[n, 1]).start()

    def space_start(n):
        pltpu.make_async_copy(core_in.at[n], core_in.at[n], core_sem.at[n, 0]).wait()
        half[n] = share[n] + core_in[n]
        for i, peer in enumerate(space_peers):
            remote(half.at[n], space_in.at[n, i], space_sem.at[n, 0], peer=peer, sent=space_sem.at[n, 1]).start()

    def factored(n, factor):
        pltpu.make_async_copy(space_in.at[n], space_in.at[n], space_sem.at[n, 0]).wait()
        terms = [half[n]] + [space_in[n, i] for i in range(len(space_peers))]
        while len(terms) > 1:
            terms = [a + b for a, b in zip(terms[::2], terms[1::2])]
        gram = terms[0]
        spread = [jnp.broadcast_to(gram[:, i : i + 1], (8, LANES)) for i in range(SLOTS)]
        gram_re = {pair: spread[SLOT_RE[pair]] for pair in PAIRS_RE}
        gram_im = {pair: spread[SLOT_IM[pair]] for pair in PAIRS_IM}
        zero = jnp.zeros((8, LANES), jnp.float32)
        up_re, up_im, inv_re, inv_im = cholesky(
            gram_re, {**gram_im, **{(j, j): zero for j in range(NB)}}
        )
        for pair in PAIRS_RE:
            inverse[SLOT_RE[pair]] = inv_re[pair]
        for pair in PAIRS_IM:
            inverse[SLOT_IM[pair]] = inv_im[pair]
        lines = zero
        for a, b in PAIRS_RE:
            lines = jnp.where(lane8 == (NB - 1 - a) * NB + b, up_re[a, b], lines)
        for a, b in PAIRS_IM:
            lines = jnp.where(lane8 == NB * NB + (NB - 1 - a) * NB + b, up_im[a, b], lines)
        return lines if factor is None else jnp.where(row8 >= SPLIT, lines, factor)

    def apply_step(f):
        co_re = {p: jnp.broadcast_to(inverse[SLOT_RE[p], pl.ds(f, 1), :], (8, LANES)) for p in PAIRS_RE}
        co_im = {p: jnp.broadcast_to(inverse[SLOT_IM[p], pl.ds(f, 1), :], (8, LANES)) for p in PAIRS_IM}
        for b in range(NB):
            for g in range(groups):
                at = pl.ds(8 * g, 8)
                total = recv[f, 0, at, :] * co_re[0, b]
                for a in range(1, b + 1):
                    total = total + recv[f, a, at, :] * co_re[a, b]
                for a in range(b):
                    total = total - turn[f, a, at, :] * co_im[a, b]
                modes[b, f, at, :] = total
        pltpu.make_async_copy(modes.at[:, f], modes_hbm.at[:, f], out_sem).start()

    pltpu.make_async_copy(recv.at[pl.ds(0, EARLY)], recv.at[pl.ds(0, EARLY)], recv_sem.at[0]).wait()
    none = jnp.zeros((8, LANES), jnp.float32)
    first = lax.fori_loop(0, EARLY, gram_step, none)
    first = lax.fori_loop(EARLY, SPLIT, waited_gram_step, first)
    core_start(0, first)
    second = waited_gram_step(SPLIT, none)
    space_start(0)
    second = lax.fori_loop(SPLIT + 1, per, waited_gram_step, second)
    core_start(1, second)
    space_start(1)
    factor = factored(0, None)
    pl.loop(0, SPLIT)(apply_step)
    factor = factored(1, factor)
    pl.loop(SPLIT, per)(apply_step)
    for f in range(per):
        line = jnp.broadcast_to(factor[f : f + 1], (8, LANES))
        for c in range(2):
            upper_half = line if c == 1 else pltpu.roll(line, LANES // 2, 1)
            factor_ref[f, c] = pltpu.roll(upper_half, NB, 1, stride=NB, stride_axis=0)[:, :NB]

    sent = spec.at[pl.ds(0, NB - 1)]
    pltpu.make_async_copy(sent, sent, send_sem).wait()
    sent = sums_in.at[pl.ds(0, NB - 1)]
    for i in range(2):
        pltpu.make_async_copy(sent, sent, small_sem.at[i]).wait()
        pltpu.make_async_copy(core_in.at[i], core_in.at[i], core_sem.at[i, 1]).wait()
        pltpu.make_async_copy(space_in.at[i], space_in.at[i], space_sem.at[i, 1]).wait()
    pltpu.make_async_copy(modes, modes_hbm, out_sem).wait()


def body(snapshots, quad_weights):
    cell_count = snapshots.shape[2]
    points = cell_count // LANES
    rows = 2 * points
    per = KF // NB
    point_total = cell_count * lax.axis_size("space")
    others = lax.axis_size("space") // 2 - 1
    x = snapshots.reshape(NFFT, 2, points, LANES).transpose(0, 2, 1, 3)
    tab, win = tables()
    f32 = jnp.float32
    anywhere = pl.BlockSpec(memory_space=pl.ANY)
    dma = pltpu.SemaphoreType.DMA
    modes, factor = pl.pallas_call(
        functools.partial(kernel, point_total),
        out_shape=(
            jax.ShapeDtypeStruct((NB, per, rows, LANES), f32),
            jax.ShapeDtypeStruct((per, 2, NB, NB), f32),
        ),
        in_specs=[anywhere] * 4,
        out_specs=(anywhere, pl.BlockSpec(memory_space=pltpu.VMEM)),
        scratch_shapes=[
            pltpu.VMEM((points, NFFT, 2, LANES), f32),
            pltpu.VMEM((4 * KF, 2 * NFFT), jnp.bfloat16),
            pltpu.VMEM((2, KF, LANES), f32),
            pltpu.VMEM((points, LANES), f32),
            pltpu.VMEM((rows, LANES), f32),
            pltpu.VMEM((NB, per, rows, LANES), f32),
            pltpu.VMEM((rows, LANES), f32),
            pltpu.VMEM((NB, 8, LANES), f32),
            pltpu.VMEM((8, LANES), f32),
            pltpu.VMEM((NB, 8, LANES), f32),
            pltpu.VMEM((per, NB, rows, LANES), f32),
            pltpu.VMEM((per, NB, rows, LANES), f32),
            pltpu.VMEM((NB, rows, LANES), f32),
            pltpu.VMEM((SLOTS * 8, LANES), f32),
            pltpu.VMEM((SLOTS, 8, LANES), f32),
            pltpu.VMEM((NB, per, rows, LANES), f32),
            pltpu.VMEM((2, 8, LANES), f32),
            pltpu.VMEM((2, 8, LANES), f32),
            pltpu.VMEM((2, 8, LANES), f32),
            pltpu.VMEM((2, others, 8, LANES), f32),
            dma((points // 4,)),
            dma((3,)),
            dma,
            dma((per,)),
            dma,
            dma,
            dma((2,)),
            dma((2, 2)),
            dma((2, 2)),
            dma,
        ],
        compiler_params=pltpu.CompilerParams(
            collective_id=0, has_side_effects=True, vmem_limit_bytes=48 * 2**20
        ),
    )(x, quad_weights.reshape(points, LANES), jnp.asarray(tab), jnp.asarray(win))
    modes = modes.reshape(NB, per, points, 2, LANES).transpose(0, 1, 3, 2, 4)
    return (modes.reshape(NB, per, 2, cell_count), factor)


def solution(mesh):
    placed = (P("tm", None, "space"), P("space"))
    return jax.shard_map(
        body,
        mesh=mesh,
        in_specs=placed,
        out_specs=(P(None, "tm", None, "space"), P("tm", None, None, None)),
        check_vma=False,
    )
```

time: 271 us -> 53.9 us (0.20); the launches traced: 267 us -> 53.7 us
  blocking collectives: 171 us -> 0 us
  Pallas kernels: 0 us -> 48.6 us
  local copies, waits for them, and re-layouts: 33.9 us -> 4.45 us
  matrix products: 21.3 us -> 0 us
  waiting for transfers between devices: 19.2 us -> 0 us
  other arithmetic: 16.7 us -> 0 us
  starting transfers between devices: 3.74 us -> 0 us
    psum x2 -> x0, blocking collectives: 171 us -> none  [the longest x1 142 us: body(): gram_re, gram_im = lax.psum(share, 'space')]
    pallas_call x0 -> x1, Pallas kernels: none -> 48.6 us  [body(): pl.pallas_call(functools.partial(kernel, point_total), out_shape=(jax.Sha...]
    dot_general x12 -> x0, matrix products: 21.3 us -> none  [the longest x1 3.79 us: transform(): jnp.einsum('kj,bjp->bkp', sin_tab, centered[:, :, 1], precision=highest)]
    all_to_all x1 -> x0, waiting for transfers between devices: 19.2 us -> none  [body(): lax.all_to_all(spectra, 'tm', split_axis=1, concat_axis=0, tiled=True)]
    another operation x62 -> x0, local copies, waits for them, and re-layouts: 17.7 us -> none  [the longest x56 14.8 us: stack_rows(): return jnp.stack([jnp.stack(entries, 0) for entries in table], 0)]
    slice x5 -> x0, local copies, waits for them, and re-layouts: 11.3 us -> none  [the longest x1 9.6 us: transform(): centered[:, :, 0]]
    sub x2 -> x0, other arithmetic: 6.41 us -> none  [the longest x1 6.37 us: body(): centered = snapshots.reshape(blocks_dev, NFFT, 2, cell_count) - time_mean]
    reduce_sum x1 -> x0, other arithmetic: 5.67 us -> none  [body(): block_total = jnp.sum(snapshots, axis=0)]
  transfers between devices with their start and end apart: 1 -> 0, of which waited for: 1 -> 0; matrix products, arithmetic and copies ran while one was open for 0% -> 0% of each run, Pallas kernels for 0% -> 0%
where the time goes in v2:
time: 53.9 us; the launch traced here: 53.7 us
  Pallas kernels  48.6 us (90%)
  local copies, waits for them, and re-layouts  4.45 us (8%)
  between operations  0.65 us (1%)
    pallas_call x1, Pallas kernels, body(): pl.pallas_call(functools.partial(kernel, point_total), out_shape=(jax.Sha...  48.6 us
    unnamed x8, local copies, waits for them, and re-layouts  4.45 us

profile of v2, /device:TPU:1, one launch (start us, length us, event | category | flops | bytes accessed | tf_op | source)
XLA Modules:
  0.0 53.7 jit_solution(10169725075596644938)
XLA Ops:
  0.6 0.0 copy-start
  0.6 0.9 %copy-done = bf16[256,512]{1,0:T(8,128)(2,1)S(1)} copy-done((bf16[256,512]{1,0:T(8,128)(2,1)S(1)}, bf16[256,512]{1,0:T(8,128)(2,1)}, u32[]{:S(2)}) %copy-start) | copy-done | bytes 262168
  1.6 0.0 copy-start.1
  1.6 0.8 %copy-done.1 = f32[2,64,128]{2,1,0:T(8,128)S(1)} copy-done((f32[2,64,128]{2,1,0:T(8,128)S(1)}, f32[2,64,128]{2,1,0:T(8,128)}, u32[]{:S(2)}) %copy-start.1) | copy-done | bytes 65560
  2.4 0.0 copy-start.2
  2.4 0.7 %copy-done.2 = f32[4096]{0:T(1024)S(1)} copy-done((f32[4096]{0:T(1024)S(1)}, f32[4096]{0:T(1024)}, u32[]{:S(2)}) %copy-start.2) | copy-done | bytes 16408
  3.1 48.6 %shard_map.59 = (f32[8,8,64,128]{3,2,1,0:T(8,128)S(1)}, f32[8,2,8,8]{3,2,1,0:T(8,128)S(1)}) custom-call(f32[256,32,2,128]{3,2,1,0:T(2,128)} %bitcast.11, f32[32,128]{1,0:T(8,128)S(1)} %bitcast.10, bf16[256,512]{1,0:T(8,128)(2,1)S(1)} %copy-done, f32[2,64,128]{2,1,0:T(8,128)S(1)} %copy-done.1), custom_call_target="tpu_custom_call" | custom-call | tf_op jit(solution)/shard_map/pallas_call | solution.py:349
  51.7 1.3 %copy.9 = f32[8,8,2,4096]{3,2,1,0:T(2,128)} copy(f32[8,8,2,4096]{3,2,1,0:T(2,128)S(1)} %bitcast.9) | data formatting | bytes 4194304
  53.0 0.6 %copy.10 = f32[8,2,8,8]{3,2,1,0:T(8,128)} copy(f32[8,2,8,8]{3,2,1,0:T(8,128)S(1)} %get-tuple-element.9) | data formatting | bytes 8192
Async XLA Ops:
  0.6 1.0 %copy-start = (bf16[256,512]{1,0:T(8,128)(2,1)S(1)}, bf16[256,512]{1,0:T(8,128)(2,1)}, u32[]{:S(2)}) copy-start(bf16[256,512]{1,0:T(8,128)(2,1)} %constant.4.clone.tab_hbm) | copy-start | bytes 786436
  1.6 0.8 %copy-start.1 = (f32[2,64,128]{2,1,0:T(8,128)S(1)}, f32[2,64,128]{2,1,0:T(8,128)}, u32[]{:S(2)}) copy-start(f32[2,64,128]{2,1,0:T(8,128)} %constant.5.clone.win_hbm) | copy-start | bytes 196612
  2.4 0.7 %copy-start.2 = (f32[4096]{0:T(1024)S(1)}, f32[4096]{0:T(1024)}, u32[]{:S(2)}) copy-start(f32[4096]{0:T(1024)} %param.5) | copy-start | bytes 49156

commit v3 on v2

--- a/solution.py
+++ b/solution.py
@@ -16,6 +16,8 @@
 LANES = 128
 EARLY = 2
 SPLIT = 6
+FILL = 3
+WINDOW = 8
 MESH = pl.DeviceIdType.MESH
 
 PAIRS_RE = [(a, b) for a in range(NB) for b in range(a, NB)]
@@ -82,10 +84,10 @@
 
 
 def kernel(
-    point_total, x_hbm, w_hbm, tab_hbm, win_hbm, modes_hbm, factor_ref,
-    xs, tab, win, wgt, wgt2, spec, sums, sums_in, mean_part, mean, recv, turn, prod, acc, inverse, modes,
+    point_total, x_hbm, w_hbm, tab_hbm, win_hbm, modes, factor_ref,
+    xs, tab, win, wgt, wgt2, spec, sums, sums_in, mean_part, mean, recv, turn, prod, acc, inverse,
     share, core_in, half, space_in,
-    x_sem, in_sem, send_sem, recv_sem, sums_sem, mean_sem, small_sem, core_sem, space_sem, out_sem,
+    x_sem, in_sem, send_sem, recv_sem, sums_sem, mean_sem, small_sem, core_sem, space_sem,
 ):
     tm = lax.axis_index("tm")
     sp = lax.axis_index("space")
@@ -192,10 +194,13 @@
             sums.at[pl.ds(pl.multiple_of(8 * mate, 8), 8)], sums_in.at[tm], sums_sem, mate=mate, sent=small_sem.at[0]
         ).start()
     pltpu.make_async_copy(sums.at[pl.ds(pl.multiple_of(8 * tm, 8), 8)], sums_in.at[tm], sums_sem).start()
-    for f in range(EARLY, per):
+    def sends(f):
         for mate in mates:
             remote(spec.at[mate, f], recv.at[f, tm], recv_sem.at[f], mate=mate).start()
         pltpu.make_async_copy(spec.at[tm, f], recv.at[f, tm], recv_sem.at[f]).start()
+
+    for f in range(EARLY, FILL):
+        sends(f)
 
     pltpu.make_async_copy(sums_in, sums_in, sums_sem).wait()
     part = sums_in[0]
@@ -205,6 +210,8 @@
     for mate in mates:
         remote(mean_part, mean.at[tm], mean_sem, mate=mate, sent=small_sem.at[1]).start()
     pltpu.make_async_copy(mean_part, mean.at[tm], mean_sem).start()
+    for f in range(FILL, WINDOW):
+        sends(f)
     wgt_copy.wait()
     scaled = wgt[...] / point_total
     wgt2[pl.ds(0, points, stride=2), :] = scaled
@@ -252,10 +259,6 @@
         )
         return jnp.where(row8 == f, line, total)
 
-    def waited_gram_step(f, total):
-        pltpu.make_async_copy(recv.at[f], recv.at[f], recv_sem.at[f]).wait()
-        return gram_step(f, total)
-
     def core_start(n, total):
         share[n] = total
         remote(share.at[n], core_in.at[n], core_sem.at[n, 0], peer=core_peer, sent=core_sem.at[n, 1]).start()
@@ -266,7 +269,7 @@
         for i, peer in enumerate(space_peers):
             remote(half.at[n], space_in.at[n, i], space_sem.at[n, 0], peer=peer, sent=space_sem.at[n, 1]).start()
 
-    def factored(n, factor):
+    def factored(n):
         pltpu.make_async_copy(space_in.at[n], space_in.at[n], space_sem.at[n, 0]).wait()
         terms = [half[n]] + [space_in[n, i] for i in range(len(space_peers))]
         while len(terms) > 1:
@@ -288,7 +291,7 @@
             lines = jnp.where(lane8 == (NB - 1 - a) * NB + b, up_re[a, b], lines)
         for a, b in PAIRS_IM:
             lines = jnp.where(lane8 == NB * NB + (NB - 1 - a) * NB + b, up_im[a, b], lines)
-        return lines if factor is None else jnp.where(row8 >= SPLIT, lines, factor)
+        return lines
 
     def apply_step(f):
         co_re = {p: jnp.broadcast_to(inverse[SLOT_RE[p], pl.ds(f, 1), :], (8, LANES)) for p in PAIRS_RE}
@@ -302,21 +305,35 @@
                 for a in range(b):
                     total = total - turn[f, a, at, :] * co_im[a, b]
                 modes[b, f, at, :] = total
-        pltpu.make_async_copy(modes.at[:, f], modes_hbm.at[:, f], out_sem).start()
 
     pltpu.make_async_copy(recv.at[pl.ds(0, EARLY)], recv.at[pl.ds(0, EARLY)], recv_sem.at[0]).wait()
-    none = jnp.zeros((8, LANES), jnp.float32)
-    first = lax.fori_loop(0, EARLY, gram_step, none)
-    first = lax.fori_loop(EARLY, SPLIT, waited_gram_step, first)
-    core_start(0, first)
-    second = waited_gram_step(SPLIT, none)
-    space_start(0)
-    second = lax.fori_loop(SPLIT + 1, per, waited_gram_step, second)
-    core_start(1, second)
+    def spectrum_step(f, total):
+        @pl.when(f >= EARLY)
+        def _():
+            pltpu.make_async_copy(recv.at[f], recv.at[f], recv_sem.at[f]).wait()
+
+        @pl.when(f + WINDOW < per)
+        def _():
+            sends(f + WINDOW)
+
+        total = gram_step(f, total)
+
+        @pl.when(f == SPLIT - 1)
+        def _():
+            core_start(0, total)
+
+        @pl.when(f == SPLIT)
+        def _():
+            space_start(0)
+
+        return total
+
+    total = lax.fori_loop(0, per, spectrum_step, jnp.zeros((8, LANES), jnp.float32))
+    core_start(1, total)
     space_start(1)
-    factor = factored(0, None)
+    factored(0)
     pl.loop(0, SPLIT)(apply_step)
-    factor = factored(1, factor)
+    factor = factored(1)
     pl.loop(SPLIT, per)(apply_step)
     for f in range(per):
         line = jnp.broadcast_to(factor[f : f + 1], (8, LANES))
@@ -331,7 +348,6 @@
         pltpu.make_async_copy(sent, sent, small_sem.at[i]).wait()
         pltpu.make_async_copy(core_in.at[i], core_in.at[i], core_sem.at[i, 1]).wait()
         pltpu.make_async_copy(space_in.at[i], space_in.at[i], space_sem.at[i, 1]).wait()
-    pltpu.make_async_copy(modes, modes_hbm, out_sem).wait()
 
 
 def body(snapshots, quad_weights):
@@ -343,8 +359,10 @@
     others = lax.axis_size("space") // 2 - 1
     x = snapshots.reshape(NFFT, 2, points, LANES).transpose(0, 2, 1, 3)
     tab, win = tables()
+    operands = (x, quad_weights.reshape(points, LANES), jnp.asarray(tab), jnp.asarray(win))
     f32 = jnp.float32
-    anywhere = pl.BlockSpec(memory_space=pl.ANY)
+    in_hbm = pl.BlockSpec(memory_space=pltpu.HBM)
+    in_vmem = pl.BlockSpec(memory_space=pltpu.VMEM)
     dma = pltpu.SemaphoreType.DMA
     modes, factor = pl.pallas_call(
         functools.partial(kernel, point_total),
@@ -352,8 +370,8 @@
             jax.ShapeDtypeStruct((NB, per, rows, LANES), f32),
             jax.ShapeDtypeStruct((per, 2, NB, NB), f32),
         ),
-        in_specs=[anywhere] * 4,
-        out_specs=(anywhere, pl.BlockSpec(memory_space=pltpu.VMEM)),
+        in_specs=[in_hbm] * 4,
+        out_specs=(in_vmem, in_vmem),
         scratch_shapes=[
             pltpu.VMEM((points, NFFT, 2, LANES), f32),
             pltpu.VMEM((4 * KF, 2 * NFFT), jnp.bfloat16),
@@ -370,7 +388,6 @@
             pltpu.VMEM((NB, rows, LANES), f32),
             pltpu.VMEM((SLOTS * 8, LANES), f32),
             pltpu.VMEM((SLOTS, 8, LANES), f32),
-            pltpu.VMEM((NB, per, rows, LANES), f32),
             pltpu.VMEM((2, 8, LANES), f32),
             pltpu.VMEM((2, 8, LANES), f32),
             pltpu.VMEM((2, 8, LANES), f32),
@@ -384,12 +401,11 @@
             dma((2,)),
             dma((2, 2)),
             dma((2, 2)),
-            dma,
         ],
         compiler_params=pltpu.CompilerParams(
             collective_id=0, has_side_effects=True, vmem_limit_bytes=48 * 2**20
         ),
-    )(x, quad_weights.reshape(points, LANES), jnp.asarray(tab), jnp.asarray(win))
+    )(*(pltpu.with_memory_space_constraint(v, pltpu.HBM) for v in operands))
     modes = modes.reshape(NB, per, points, 2, LANES).transpose(0, 1, 3, 2, 4)
     return (modes.reshape(NB, per, 2, cell_count), factor)
 

time: 53.9 us -> 48.8 us (0.905)
  local copies, waits for them, and re-layouts: 4.45 us -> 1.95 us
  Pallas kernels: 48.6 us -> 46.2 us
    unnamed x8 -> x2, local copies, waits for them, and re-layouts: 4.45 us -> 1.95 us
    pallas_call x1, Pallas kernels: 48.6 us -> 46.2 us  [body(): pl.pallas_call(functools.partial(kernel, point_total), out_shape=(jax.Sha...]
where the time goes in v3:
time: 48.8 us
  Pallas kernels  46.2 us (95%)
  local copies, waits for them, and re-layouts  1.95 us (4%)
  between operations  0.64 us (1%)
    pallas_call x1, Pallas kernels, body(): pl.pallas_call(functools.partial(kernel, point_total), out_shape=(jax.Sha...  46.2 us
    unnamed x2, local copies, waits for them, and re-layouts  1.95 us

profile of v3, /device:TPU:1, one launch (start us, length us, event | category | flops | bytes accessed | tf_op | source)
XLA Modules:
  0.0 48.8 jit_solution(9938619171307386767)
XLA Ops:
  0.6 46.2 %shard_map.59 = (f32[8,8,64,128]{3,2,1,0:T(8,128)S(1)}, f32[8,2,8,8]{3,2,1,0:T(8,128)S(1)}) custom-call(f32[256,32,2,128]{3,2,1,0:T(2,128)} %bitcast.10, f32[32,128]{1,0:T(8,128)} %bitcast.11, bf16[256,512]{1,0:T(8,128)(2,1)} %constant.4.clone.tab_hbm, f32[2,64,128]{2,1,0:T(8,128)} %constant.5.clone.win_hbm), custom_call_target="tpu_custom_call" | custom-call | tf_op jit(solution)/shard_map/pallas_call | solution.py:367
  46.8 1.3 %copy.9 = f32[8,8,2,4096]{3,2,1,0:T(2,128)} copy(f32[8,8,2,4096]{3,2,1,0:T(2,128)S(1)} %bitcast.9) | data formatting | bytes 4194304
  48.1 0.6 %copy.10 = f32[8,2,8,8]{3,2,1,0:T(8,128)} copy(f32[8,2,8,8]{3,2,1,0:T(8,128)S(1)} %get-tuple-element.9) | data formatting | bytes 8192

commit v4 on v3

--- a/solution.py
+++ b/solution.py
@@ -14,9 +14,9 @@
 NFFT = 256
 KF = 64
 LANES = 128
-EARLY = 2
+EARLY = 3
 SPLIT = 6
-FILL = 3
+FILL = 4
 WINDOW = 8
 MESH = pl.DeviceIdType.MESH
 
@@ -99,15 +99,20 @@
     z_hi, y, core = lax.div(sp, 8), lax.rem(lax.div(sp, 2), 4), lax.rem(sp, 2)
     mates = [lax.rem(tm + d, NB) for d in range(1, NB)]
     core_peer = z_hi * 8 + y * 2 + (1 - core)
+    around = [(dz, dy) for dz in range(4) for dy in range(4) if (dz, dy) != (0, 0)]
+    around.sort(key=lambda way: -2 * min(way[0], 4 - way[0]) - min(way[1], 4 - way[1]))
     space_peers = [
-        lax.rem(z_hi + dz, 4) * 8 + lax.rem(y + dy, 4) * 2 + core
-        for dz in range(4)
-        for dy in range(4)
-        if (dz, dy) != (0, 0)
+        lax.rem(z_hi + dz, 4) * 8 + lax.rem(y + dy, 4) * 2 + core for dz, dy in around
     ]
 
     def x_copy(pt):
         return pltpu.make_async_copy(x_hbm.at[:, pt], xs.at[pt], x_sem.at[pt // 4])
+
+    barrier = pltpu.get_barrier_semaphore()
+    for peer in [*space_peers, core_peer]:
+        pl.semaphore_signal(barrier, 1, device_id=(tm, peer), device_id_type=MESH)
+    for mate in mates:
+        pl.semaphore_signal(barrier, 1, device_id=(mate, sp), device_id_type=MESH)
 
     tab_copy = pltpu.make_async_copy(tab_hbm, tab, in_sem.at[0])
     win_copy = pltpu.make_async_copy(win_hbm, win, in_sem.at[1])
@@ -119,12 +124,6 @@
     for pt in range(4, points):
         x_copy(pt).start()
     wgt_copy.start()
-
-    barrier = pltpu.get_barrier_semaphore()
-    for mate in mates:
-        pl.semaphore_signal(barrier, 1, device_id=(mate, sp), device_id_type=MESH)
-    for peer in [core_peer, *space_peers]:
-        pl.semaphore_signal(barrier, 1, device_id=(tm, peer), device_id_type=MESH)
 
     row8 = lax.broadcasted_iota(jnp.int32, (8, LANES), 0)
     lane8 = lax.broadcasted_iota(jnp.int32, (8, LANES), 1)
@@ -177,23 +176,31 @@
                 spec.at[mate, pl.ds(0, EARLY), at], recv.at[pl.ds(0, EARLY), tm, at], recv_sem.at[0], mate=mate
             ).start()
 
+    def sums_send(q):
+        part = sums.at[pl.ds(pl.multiple_of(8 * q, 8), 8)]
+
+        @pl.when(tm != q)
+        def _():
+            remote(part, sums_in.at[tm], sums_sem, mate=q, sent=small_sem.at[0]).start()
+
+        @pl.when(tm == q)
+        def _():
+            pltpu.make_async_copy(part, sums_in.at[tm], sums_sem).start()
+
     tab_copy.wait()
     win_copy.wait()
     transform_step(0)
     pl.semaphore_wait(barrier, len(mates) + 1 + len(space_peers))
+    sums_send(0)
     early_sends(0)
 
     @pl.loop(1, steps)
     def _(q):
         transform_step(q)
+        sums_send(q)
         early_sends(q)
 
     pltpu.make_async_copy(spec.at[tm, pl.ds(0, EARLY)], recv.at[pl.ds(0, EARLY), tm], recv_sem.at[0]).start()
-    for mate in mates:
-        remote(
-            sums.at[pl.ds(pl.multiple_of(8 * mate, 8), 8)], sums_in.at[tm], sums_sem, mate=mate, sent=small_sem.at[0]
-        ).start()
-    pltpu.make_async_copy(sums.at[pl.ds(pl.multiple_of(8 * tm, 8), 8)], sums_in.at[tm], sums_sem).start()
     def sends(f):
         for mate in mates:
             remote(spec.at[mate, f], recv.at[f, tm], recv_sem.at[f], mate=mate).start()
@@ -348,6 +355,15 @@
         pltpu.make_async_copy(sent, sent, small_sem.at[i]).wait()
         pltpu.make_async_copy(core_in.at[i], core_in.at[i], core_sem.at[i, 1]).wait()
         pltpu.make_async_copy(space_in.at[i], space_in.at[i], space_sem.at[i, 1]).wait()
+
+
+def writer(modes, factor, modes_out, factor_out, sem):
+    copies = [pltpu.make_async_copy(modes.at[b], modes_out.at[b], sem.at[b]) for b in range(NB)]
+    copies.append(pltpu.make_async_copy(factor, factor_out, sem.at[NB]))
+    for copy in copies:
+        copy.start()
+    for copy in copies:
+        copy.wait()
 
 
 def body(snapshots, quad_weights):
@@ -406,6 +422,14 @@
             collective_id=0, has_side_effects=True, vmem_limit_bytes=48 * 2**20
         ),
     )(*(pltpu.with_memory_space_constraint(v, pltpu.HBM) for v in operands))
+    modes, factor = pl.pallas_call(
+        writer,
+        out_shape=(jax.ShapeDtypeStruct(modes.shape, f32), jax.ShapeDtypeStruct(factor.shape, f32)),
+        in_specs=[in_vmem] * 2,
+        out_specs=(in_hbm, in_hbm),
+        scratch_shapes=[dma((NB + 1,))],
+        compiler_params=pltpu.CompilerParams(vmem_limit_bytes=8 * 2**20),
+    )(modes, factor)
     modes = modes.reshape(NB, per, points, 2, LANES).transpose(0, 1, 3, 2, 4)
     return (modes.reshape(NB, per, 2, cell_count), factor)
 

time: 48.8 us -> 48.4 us (level)
  local copies, waits for them, and re-layouts: 1.95 us -> 0 us
  Pallas kernels: 46.2 us -> 47.6 us
    unnamed x2 -> x0, local copies, waits for them, and re-layouts: 1.95 us -> none
    pallas_call x0 -> x1, Pallas kernels: none -> 1.4 us  [body(): pl.pallas_call(writer, out_shape=(jax.ShapeDtypeStruct(modes.shape, f32),...]
where the time goes in v4:
time: 48.4 us; the launch traced here: 48.3 us
  Pallas kernels  47.6 us (98%)
  between operations  0.64 us (1%)
    pallas_call x1, Pallas kernels, body(): pl.pallas_call(functools.partial(kernel, point_total), out_shape=(jax.Sha...  46.2 us
    pallas_call x1, Pallas kernels, body(): pl.pallas_call(writer, out_shape=(jax.ShapeDtypeStruct(modes.shape, f32),...  1.4 us

profile of v4, /device:TPU:1, one launch (start us, length us, event | category | flops | bytes accessed | tf_op | source)
XLA Modules:
  0.0 48.3 jit_solution(2234650408656605196)
XLA Ops:
  0.6 46.2 %shard_map.59 = (f32[8,8,64,128]{3,2,1,0:T(8,128)S(1)}, f32[8,2,8,8]{3,2,1,0:T(8,128)S(1)}) custom-call(f32[256,32,2,128]{3,2,1,0:T(2,128)} %bitcast.9, f32[32,128]{1,0:T(8,128)} %bitcast.10, bf16[256,512]{1,0:T(8,128)(2,1)} %constant.4.clone.tab_hbm, f32[2,64,128]{2,1,0:T(8,128)} %constant.5.clone.win_hbm), custom_call_target="tpu_custom_call" | custom-call | tf_op jit(solution)/shard_map/pallas_call | solution.py:383
  46.9 1.4 %shard_map.60 = (f32[8,8,64,128]{3,2,1,0:T(8,128)}, f32[8,2,8,8]{3,2,1,0:T(8,128)}) custom-call(f32[8,8,64,128]{3,2,1,0:T(8,128)S(1)} %get-tuple-element.6.modes, f32[8,2,8,8]{3,2,1,0:T(8,128)S(1)} %get-tuple-element.7.factor), custom_call_target="tpu_custom_call" | custom-call | tf_op jit(solution)/shard_map/pallas_call | solution.py:425

commit v5 on v4

--- a/solution.py
+++ b/solution.py
@@ -86,9 +86,11 @@
 def kernel(
     point_total, x_hbm, w_hbm, tab_hbm, win_hbm, modes, factor_ref,
     xs, tab, win, wgt, wgt2, spec, sums, sums_in, mean_part, mean, recv, turn, prod, acc, inverse,
-    share, core_in, half, space_in,
+    share_0, share_1, core_in_0, core_in_1, half_0, half_1, space_in_0, space_in_1,
     x_sem, in_sem, send_sem, recv_sem, sums_sem, mean_sem, small_sem, core_sem, space_sem,
 ):
+    share, core_in = (share_0, share_1), (core_in_0, core_in_1)
+    half, space_in = (half_0, half_1), (space_in_0, space_in_1)
     tm = lax.axis_index("tm")
     sp = lax.axis_index("space")
     points = xs.shape[0]
@@ -267,21 +269,24 @@
         return jnp.where(row8 == f, line, total)
 
     def core_start(n, total):
-        share[n] = total
-        remote(share.at[n], core_in.at[n], core_sem.at[n, 0], peer=core_peer, sent=core_sem.at[n, 1]).start()
+        share[n][...] = total
+        remote(share[n], core_in[n], core_sem.at[n, 0], peer=core_peer, sent=core_sem.at[n, 1]).start()
 
     def space_start(n):
-        pltpu.make_async_copy(core_in.at[n], core_in.at[n], core_sem.at[n, 0]).wait()
-        half[n] = share[n] + core_in[n]
+        pltpu.make_async_copy(core_in[n], core_in[n], core_sem.at[n, 0]).wait()
+        half[n][...] = share[n][...] + core_in[n][...]
         for i, peer in enumerate(space_peers):
-            remote(half.at[n], space_in.at[n, i], space_sem.at[n, 0], peer=peer, sent=space_sem.at[n, 1]).start()
+            remote(half[n], space_in[n].at[i], space_sem.at[n, 0], peer=peer, sent=space_sem.at[n, 1]).start()
 
     def factored(n):
-        pltpu.make_async_copy(space_in.at[n], space_in.at[n], space_sem.at[n, 0]).wait()
-        terms = [half[n]] + [space_in[n, i] for i in range(len(space_peers))]
+        pltpu.make_async_copy(space_in[n], space_in[n], space_sem.at[n, 0]).wait()
+        terms = [half[n][...]] + [space_in[n][i] for i in range(len(space_peers))]
         while len(terms) > 1:
             terms = [a + b for a, b in zip(terms[::2], terms[1::2])]
         gram = terms[0]
+        if n == 1:
+            gram = jnp.broadcast_to(gram, (8, LANES))
+            gram = jnp.where(row8 == per - 1, pltpu.roll(gram, SLOTS, 1), gram)
         spread = [jnp.broadcast_to(gram[:, i : i + 1], (8, LANES)) for i in range(SLOTS)]
         gram_re = {pair: spread[SLOT_RE[pair]] for pair in PAIRS_RE}
         gram_im = {pair: spread[SLOT_IM[pair]] for pair in PAIRS_IM}
@@ -336,11 +341,11 @@
         return total
 
     total = lax.fori_loop(0, per, spectrum_step, jnp.zeros((8, LANES), jnp.float32))
-    core_start(1, total)
+    core_start(1, total[SPLIT : SPLIT + 1] + pltpu.roll(total, SLOTS, 1)[per - 1 :])
     space_start(1)
-    factored(0)
+    factor = factored(0)
     pl.loop(0, SPLIT)(apply_step)
-    factor = factored(1)
+    factor = jnp.where(row8 < SPLIT, factor, factored(1))
     pl.loop(SPLIT, per)(apply_step)
     for f in range(per):
         line = jnp.broadcast_to(factor[f : f + 1], (8, LANES))
@@ -353,8 +358,8 @@
     sent = sums_in.at[pl.ds(0, NB - 1)]
     for i in range(2):
         pltpu.make_async_copy(sent, sent, small_sem.at[i]).wait()
-        pltpu.make_async_copy(core_in.at[i], core_in.at[i], core_sem.at[i, 1]).wait()
-        pltpu.make_async_copy(space_in.at[i], space_in.at[i], space_sem.at[i, 1]).wait()
+        pltpu.make_async_copy(core_in[i], core_in[i], core_sem.at[i, 1]).wait()
+        pltpu.make_async_copy(space_in[i], space_in[i], space_sem.at[i, 1]).wait()
 
 
 def writer(modes, factor, modes_out, factor_out, sem):
@@ -404,10 +409,14 @@
             pltpu.VMEM((NB, rows, LANES), f32),
             pltpu.VMEM((SLOTS * 8, LANES), f32),
             pltpu.VMEM((SLOTS, 8, LANES), f32),
-            pltpu.VMEM((2, 8, LANES), f32),
-            pltpu.VMEM((2, 8, LANES), f32),
-            pltpu.VMEM((2, 8, LANES), f32),
-            pltpu.VMEM((2, others, 8, LANES), f32),
+            pltpu.VMEM((8, LANES), f32),
+            pltpu.VMEM((1, LANES), f32),
+            pltpu.VMEM((8, LANES), f32),
+            pltpu.VMEM((1, LANES), f32),
+            pltpu.VMEM((8, LANES), f32),
+            pltpu.VMEM((1, LANES), f32),
+            pltpu.VMEM((others, 8, LANES), f32),
+            pltpu.VMEM((others, 1, LANES), f32),
             dma((points // 4,)),
             dma((3,)),
             dma,

time: 48.4 us -> 48.1 us (level)
  no operation moved by 1% of the time
where the time goes in v5:
time: 48.1 us; the launch traced here: 48 us
  Pallas kernels  47.4 us (99%)
  between operations  0.64 us (1%)
    pallas_call x1, Pallas kernels, body(): pl.pallas_call(functools.partial(kernel, point_total), out_shape=(jax.Sha...  46 us
    pallas_call x1, Pallas kernels, body(): pl.pallas_call(writer, out_shape=(jax.ShapeDtypeStruct(modes.shape, f32),...  1.4 us

profile of v5, /device:TPU:1, one launch (start us, length us, event | category | flops | bytes accessed | tf_op | source)
XLA Modules:
  0.0 48.0 jit_solution(17822690996809116738)
XLA Ops:
  0.6 46.0 %shard_map.59 = (f32[8,8,64,128]{3,2,1,0:T(8,128)S(1)}, f32[8,2,8,8]{3,2,1,0:T(8,128)S(1)}) custom-call(f32[256,32,2,128]{3,2,1,0:T(2,128)} %bitcast.9, f32[32,128]{1,0:T(8,128)} %bitcast.10, bf16[256,512]{1,0:T(8,128)(2,1)} %constant.4.clone.tab_hbm, f32[2,64,128]{2,1,0:T(8,128)} %constant.5.clone.win_hbm), custom_call_target="tpu_custom_call" | custom-call | tf_op jit(solution)/shard_map/pallas_call | solution.py:388
  46.6 1.4 %shard_map.60 = (f32[8,8,64,128]{3,2,1,0:T(8,128)}, f32[8,2,8,8]{3,2,1,0:T(8,128)}) custom-call(f32[8,8,64,128]{3,2,1,0:T(8,128)S(1)} %get-tuple-element.6.modes, f32[8,2,8,8]{3,2,1,0:T(8,128)S(1)} %get-tuple-element.7.factor), custom_call_target="tpu_custom_call" | custom-call | tf_op jit(solution)/shard_map/pallas_call | solution.py:434

commit v6 on v5

--- a/solution.py
+++ b/solution.py
@@ -99,7 +99,8 @@
     per = KF // NB
 
     z_hi, y, core = lax.div(sp, 8), lax.rem(lax.div(sp, 2), 4), lax.rem(sp, 2)
-    mates = [lax.rem(tm + d, NB) for d in range(1, NB)]
+    near_first = [(0, 1), (1, 0), (3, 0), (1, 1), (3, 1), (2, 0), (2, 1)]
+    mates = [lax.rem(lax.div(tm, 2) + dx, 4) * 2 + lax.rem(tm + dz, 2) for dx, dz in near_first]
     core_peer = z_hi * 8 + y * 2 + (1 - core)
     around = [(dz, dy) for dz in range(4) for dy in range(4) if (dz, dy) != (0, 0)]
     around.sort(key=lambda way: -2 * min(way[0], 4 - way[0]) - min(way[1], 4 - way[1]))

time: 48.1 us -> 49.1 us (1.021)
  Pallas kernels: 47.4 us -> 48.3 us
    pallas_call x1, Pallas kernels: 46 us -> 46.9 us  [body(): pl.pallas_call(functools.partial(kernel, point_total), out_shape=(jax.Sha...]
where the time goes in v6:
time: 49.1 us; the launch traced here: 49 us
  Pallas kernels  48.3 us (98%)
  between operations  0.64 us (1%)
    pallas_call x1, Pallas kernels, body(): pl.pallas_call(functools.partial(kernel, point_total), out_shape=(jax.Sha...  46.9 us
    pallas_call x1, Pallas kernels, body(): pl.pallas_call(writer, out_shape=(jax.ShapeDtypeStruct(modes.shape, f32),...  1.4 us

profile of v6, /device:TPU:1, one launch (start us, length us, event | category | flops | bytes accessed | tf_op | source)
XLA Modules:
  0.0 49.0 jit_solution(9106932751653607002)
XLA Ops:
  0.6 46.9 %shard_map.59 = (f32[8,8,64,128]{3,2,1,0:T(8,128)S(1)}, f32[8,2,8,8]{3,2,1,0:T(8,128)S(1)}) custom-call(f32[256,32,2,128]{3,2,1,0:T(2,128)} %bitcast.9, f32[32,128]{1,0:T(8,128)} %bitcast.10, bf16[256,512]{1,0:T(8,128)(2,1)} %constant.4.clone.tab_hbm, f32[2,64,128]{2,1,0:T(8,128)} %constant.5.clone.win_hbm), custom_call_target="tpu_custom_call" | custom-call | tf_op jit(solution)/shard_map/pallas_call | solution.py:389
  47.6 1.4 %shard_map.60 = (f32[8,8,64,128]{3,2,1,0:T(8,128)}, f32[8,2,8,8]{3,2,1,0:T(8,128)}) custom-call(f32[8,8,64,128]{3,2,1,0:T(8,128)S(1)} %get-tuple-element.6.modes, f32[8,2,8,8]{3,2,1,0:T(8,128)S(1)} %get-tuple-element.7.factor), custom_call_target="tpu_custom_call" | custom-call | tf_op jit(solution)/shard_map/pallas_call | solution.py:435
